TPU v7x, 32 devices: a whole 2x2x4 slice. The times are simulated.
32 devices in a mesh: dp: 32 (over z, y, x, core).
Axes of the slice: x: 2, y: 2, z: 4, core: 2. Of those that a mesh axis runs over, the one named last changes fastest.
Arguments:
- tokens: bfloat16 [65536, 512], P('dp'), may hold values from -6 to 6
- segment: int32 [65536], P('dp'), may hold values from 0 to 2, as said below
- counts: int32 [32], P('dp'), may hold values from 1024 to 2048, as said below
- memory: bfloat16 [20, 512], P(None, 'dp'), may hold values from -6 to 6
- w_query: bfloat16 [512, 512], P('dp'), may hold values from -0.375 to 0.375
- b_query: bfloat16 [512], P('dp'), may hold values from -3 to 3
- w_key: bfloat16 [512, 512], P('dp'), may hold values from -0.25 to 0.25
- w_value: bfloat16 [512, 512], P('dp'), may hold values from -0.25 to 0.25
- b_value: bfloat16 [512], P('dp'), may hold values from -3 to 3
- w_out: bfloat16 [512, 512], P('dp'), may hold values from -1 to 1
- b_out: bfloat16 [512], P('dp'), may hold values from -3 to 3
- gain_attn: bfloat16 [512], P('dp'), may hold values from 0.5 to 1.5
- shift_attn: bfloat16 [512], P('dp'), may hold values from -3 to 3
- w_up: bfloat16 [512, 2048], P('dp'), may hold values from -0.25 to 0.25
- b_up: bfloat16 [2048], P('dp'), may hold values from -3 to 3
- w_down: bfloat16 [2048, 512], P('dp'), may hold values from -0.125 to 0.125
- b_down: bfloat16 [512], P('dp'), may hold values from -3 to 3
- gain_ffn: bfloat16 [512], P('dp'), may hold values from 0.5 to 1.5
- shift_ffn: bfloat16 [512], P('dp'), may hold values from -3 to 3
- cotangent: bfloat16 [65536, 512], P('dp'), may hold values from -6 to 6
Outputs:
- output: bfloat16 [65536, 512], P('dp')
- grad_tokens: float32 [65536, 512], P('dp')
- grad_memory: float32 [20, 512], P(None, 'dp')
- grad_w_query: float32 [512, 512], P('dp')
- grad_b_query: float32 [512], P('dp')
- grad_w_key: float32 [512, 512], P('dp')
- grad_w_value: float32 [512, 512], P('dp')
- grad_b_value: float32 [512], P('dp')
- grad_w_out: float32 [512, 512], P('dp')
- grad_b_out: float32 [512], P('dp')
- grad_gain_attn: float32 [512], P('dp')
- grad_shift_attn: float32 [512], P('dp')
- grad_w_up: float32 [512, 2048], P('dp')
- grad_b_up: float32 [2048], P('dp')
- grad_w_down: float32 [2048, 512], P('dp')
- grad_b_down: float32 [512], P('dp')
- grad_gain_ffn: float32 [512], P('dp')
- grad_shift_ffn: float32 [512], P('dp')
Inputs may be any that keep to these rules, and one draw needn't show every extreme that they name: `segment`: within each device's 2048 slots the ids never fall and each id marks one sequence; every used sequence has 128 to 1024 slots; in every draw some device holds a used sequence of exactly 1024 tokens. Ids past a device's used count carry no meaning. `counts`: slots are used from the start of each device and end where a sequence ends; in every draw some device uses all 2048 and some device uses 1024.
All inputs are finite; a program needn't handle non-finite values.
Results may differ from a plain program's by a relative error of at most 0.015.
The roundings to bfloat16 on the way count: a program that leaves them out, or rounds other values in their place, can miss the bound.
Values may be sent and summed in bfloat16 or wider, within the bound.
A program may use at most 320 MiB of HBM per device.

v0:
```python
import jax
import jax.numpy as jnp
from jax import lax
from jax.sharding import PartitionSpec as P

H = 8
HD = 64
QB = 512
EPS = 1e-05
NEG = -1e30


def normalize(value, gain):
    mean = jnp.mean(value, axis=-1, keepdims=True)
    centred = value - mean
    spread = jnp.mean(centred * centred, axis=-1, keepdims=True)
    return centred * lax.rsqrt(spread + EPS) * gain


def smooth(value):
    return jax.nn.gelu(value, approximate=False)


def matmul(left, right):
    return jnp.dot(left, right, preferred_element_type=jnp.float32)


def grad_weight(left, right):
    return lax.dot_general(
        left, right, (((0,), (0,)), ((), ())), preferred_element_type=jnp.float32
    )


def grad_input(left, right):
    return lax.dot_general(
        left, right, (((1,), (1,)), ((), ())), preferred_element_type=jnp.float32
    )


def column_sum(value):
    return jnp.sum(value.astype(jnp.float32), axis=0)


def shards(
    tokens,
    segment,
    counts,
    memory,
    w_query,
    b_query,
    w_key,
    w_value,
    b_value,
    w_out,
    b_out,
    gain_attn,
    shift_attn,
    w_up,
    b_up,
    w_down,
    b_down,
    gain_ffn,
    shift_ffn,
    cotangent,
):
    full = (
        lax.all_gather(memory, "dp", axis=1, tiled=True),
        lax.all_gather(w_query, "dp", axis=0, tiled=True),
        lax.all_gather(b_query, "dp", axis=0, tiled=True),
        lax.all_gather(w_key, "dp", axis=0, tiled=True),
        lax.all_gather(w_value, "dp", axis=0, tiled=True),
        lax.all_gather(b_value, "dp", axis=0, tiled=True),
        lax.all_gather(w_out, "dp", axis=0, tiled=True),
        lax.all_gather(b_out, "dp", axis=0, tiled=True),
        lax.all_gather(gain_attn, "dp", axis=0, tiled=True),
        lax.all_gather(shift_attn, "dp", axis=0, tiled=True),
        lax.all_gather(w_up, "dp", axis=0, tiled=True),
        lax.all_gather(b_up, "dp", axis=0, tiled=True),
        lax.all_gather(w_down, "dp", axis=0, tiled=True),
        lax.all_gather(b_down, "dp", axis=0, tiled=True),
        lax.all_gather(gain_ffn, "dp", axis=0, tiled=True),
        lax.all_gather(shift_ffn, "dp", axis=0, tiled=True),
    )
    (
        memory_full,
        query_weight,
        query_bias,
        key_weight,
        value_weight,
        value_bias,
        out_weight,
        out_bias,
        gain_one,
        shift_one,
        up_weight,
        up_bias,
        down_weight,
        down_bias,
        gain_two,
        shift_two,
    ) = full
    slots = tokens.shape[0]
    width = tokens.shape[1]
    memory_rows = memory_full.shape[0]
    blocks = slots // QB
    scale = HD ** (-0.5)
    valid = jnp.arange(slots) < counts[0]
    key_seg = jnp.where(valid, segment, -1)
    queries = (matmul(tokens, query_weight) + query_bias.astype(jnp.float32)).astype(jnp.bfloat16)
    keys_tok = matmul(tokens, key_weight).astype(jnp.bfloat16)
    keys_mem = matmul(memory_full, key_weight).astype(jnp.bfloat16)
    values_tok = (matmul(tokens, value_weight) + value_bias.astype(jnp.float32)).astype(
        jnp.bfloat16
    )
    values_mem = (matmul(memory_full, value_weight) + value_bias.astype(jnp.float32)).astype(
        jnp.bfloat16
    )
    key_heads = keys_tok.reshape(slots, H, HD)
    key_mem_heads = keys_mem.reshape(memory_rows, H, HD)
    value_heads = values_tok.reshape(slots, H, HD)
    value_mem_heads = values_mem.reshape(memory_rows, H, HD)
    query_blocks = queries.reshape(blocks, QB, H, HD)
    seg_blocks = segment.reshape(blocks, QB)

    def score_block(query_block, seg_block):
        tok_scores = (
            jnp.einsum("qhd,khd->hqk", query_block, key_heads, preferred_element_type=jnp.float32)
            * scale
        )
        mem_scores = (
            jnp.einsum(
                "qhd,khd->hqk", query_block, key_mem_heads, preferred_element_type=jnp.float32
            )
            * scale
        )
        allowed = key_seg[None, :] == seg_block[:, None]
        return (jnp.where(allowed[None], tok_scores, NEG), mem_scores)

    def forward_block(item):
        query_block, seg_block = item
        tok_scores, mem_scores = score_block(query_block, seg_block)
        top = jnp.maximum(jnp.max(tok_scores, axis=-1), jnp.max(mem_scores, axis=-1))
        tok_exp = jnp.exp(tok_scores - top[..., None])
        mem_exp = jnp.exp(mem_scores - top[..., None])
        total = jnp.sum(tok_exp, axis=-1) + jnp.sum(mem_exp, axis=-1)
        tok_weights = (tok_exp / total[..., None]).astype(jnp.bfloat16)
        mem_weights = (mem_exp / total[..., None]).astype(jnp.bfloat16)
        mixed_block = jnp.einsum(
            "hqk,khd->qhd", tok_weights, value_heads, preferred_element_type=jnp.float32
        )
        mixed_block = mixed_block + jnp.einsum(
            "hqk,khd->qhd", mem_weights, value_mem_heads, preferred_element_type=jnp.float32
        )
        return (mixed_block.astype(jnp.bfloat16), top + jnp.log(total))

    mixed_blocks, log_totals = lax.map(forward_block, (query_blocks, seg_blocks))
    mixed = mixed_blocks.reshape(slots, width)
    attention = matmul(mixed, out_weight) + out_bias.astype(jnp.float32)
    first_sum = tokens.astype(jnp.float32) + attention
    first = normalize(first_sum, gain_one.astype(jnp.float32)) + shift_one.astype(jnp.float32)
    first_low = first.astype(jnp.bfloat16)
    hidden = matmul(first_low, up_weight) + up_bias.astype(jnp.float32)
    active = smooth(hidden).astype(jnp.bfloat16)
    branch = matmul(active, down_weight) + down_bias.astype(jnp.float32)
    second_sum = first + branch
    result = normalize(second_sum, gain_two.astype(jnp.float32)) + shift_two.astype(jnp.float32)
    output = jnp.where(valid[:, None], result, 0.0).astype(jnp.bfloat16)
    again = (
        lax.all_gather(memory, "dp", axis=1, tiled=True),
        lax.all_gather(w_query, "dp", axis=0, tiled=True),
        lax.all_gather(w_key, "dp", axis=0, tiled=True),
        lax.all_gather(w_value, "dp", axis=0, tiled=True),
        lax.all_gather(w_out, "dp", axis=0, tiled=True),
        lax.all_gather(w_up, "dp", axis=0, tiled=True),
        lax.all_gather(w_down, "dp", axis=0, tiled=True),
        lax.all_gather(gain_attn, "dp", axis=0, tiled=True),
        lax.all_gather(gain_ffn, "dp", axis=0, tiled=True),
    )
    (
        memory_back,
        query_back,
        key_back,
        value_back,
        out_back,
        up_back,
        down_back,
        gain_one_back,
        gain_two_back,
    ) = again
    seed_grad = jnp.where(valid[:, None], cotangent.astype(jnp.float32), 0.0)
    unused_two, second_back = jax.vjp(normalize, second_sum, gain_two_back.astype(jnp.float32))
    grad_second, grad_gain_two = second_back(seed_grad)
    grad_shift_two = jnp.sum(seed_grad, axis=0)
    branch_grad = grad_second.astype(jnp.bfloat16)
    grad_down = grad_weight(active, branch_grad)
    grad_down_bias = column_sum(branch_grad)
    active_grad = grad_input(branch_grad, down_back)
    unused_hidden, smooth_back = jax.vjp(smooth, hidden)
    hidden_grad = smooth_back(active_grad)[0].astype(jnp.bfloat16)
    grad_up = grad_weight(first_low, hidden_grad)
    grad_up_bias = column_sum(hidden_grad)
    first_grad = grad_second + grad_input(hidden_grad, up_back)
    unused_one, first_back = jax.vjp(normalize, first_sum, gain_one_back.astype(jnp.float32))
    grad_first_sum, grad_gain_one = first_back(first_grad)
    grad_shift_one = jnp.sum(first_grad, axis=0)
    attention_grad = grad_first_sum.astype(jnp.bfloat16)
    grad_out = grad_weight(mixed, attention_grad)
    grad_out_bias = column_sum(attention_grad)
    mixed_grad = grad_input(attention_grad, out_back).astype(jnp.bfloat16)
    grad_blocks = mixed_grad.reshape(blocks, QB, H, HD)

    def backward_block(carry, item):
        key_tok_acc, value_tok_acc, key_mem_acc, value_mem_acc = carry
        query_block, grad_block, total_block, seg_block = item
        tok_scores, mem_scores = score_block(query_block, seg_block)
        tok_probs = jnp.exp(tok_scores - total_block[..., None])
        mem_probs = jnp.exp(mem_scores - total_block[..., None])
        tok_dprobs = jnp.einsum(
            "qhd,khd->hqk", grad_block, value_heads, preferred_element_type=jnp.float32
        )
        mem_dprobs = jnp.einsum(
            "qhd,khd->hqk", grad_block, value_mem_heads, preferred_element_type=jnp.float32
        )
        centre = jnp.sum(tok_probs * tok_dprobs, axis=-1) + jnp.sum(mem_probs * mem_dprobs, axis=-1)
        tok_sgrad = (tok_probs * (tok_dprobs - centre[..., None])).astype(jnp.bfloat16)
        mem_sgrad = (mem_probs * (mem_dprobs - centre[..., None])).astype(jnp.bfloat16)
        query_part = jnp.einsum(
            "hqk,khd->qhd", tok_sgrad, key_heads, preferred_element_type=jnp.float32
        )
        query_part = (
            query_part
            + jnp.einsum(
                "hqk,khd->qhd", mem_sgrad, key_mem_heads, preferred_element_type=jnp.float32
            )
        ) * scale
        key_tok_acc = (
            key_tok_acc
            + jnp.einsum("hqk,qhd->khd", tok_sgrad, query_block, preferred_element_type=jnp.float32)
            * scale
        )
        key_mem_acc = (
            key_mem_acc
            + jnp.einsum("hqk,qhd->khd", mem_sgrad, query_block, preferred_element_type=jnp.float32)
            * scale
        )
        value_tok_acc = value_tok_acc + jnp.einsum(
            "hqk,qhd->khd",
            tok_probs.astype(jnp.bfloat16),
            grad_block,
            preferred_element_type=jnp.float32,
        )
        value_mem_acc = value_mem_acc + jnp.einsum(
            "hqk,qhd->khd",
            mem_probs.astype(jnp.bfloat16),
            grad_block,
            preferred_element_type=jnp.float32,
        )
        return (
            (key_tok_acc, value_tok_acc, key_mem_acc, value_mem_acc),
            query_part.astype(jnp.bfloat16),
        )

    start = (
        jnp.zeros((slots, H, HD), jnp.float32),
        jnp.zeros((slots, H, HD), jnp.float32),
        jnp.zeros((memory_rows, H, HD), jnp.float32),
        jnp.zeros((memory_rows, H, HD), jnp.float32),
    )
    sums, query_parts = lax.scan(
        backward_block, start, (query_blocks, grad_blocks, log_totals, seg_blocks)
    )
    key_tok_grad = sums[0].reshape(slots, width).astype(jnp.bfloat16)
    value_tok_grad = sums[1].reshape(slots, width).astype(jnp.bfloat16)
    key_mem_grad = sums[2].reshape(memory_rows, width).astype(jnp.bfloat16)
    value_mem_grad = sums[3].reshape(memory_rows, width).astype(jnp.bfloat16)
    query_grad = query_parts.reshape(slots, width)
    grad_query = grad_weight(tokens, query_grad)
    grad_query_bias = column_sum(query_grad)
    grad_key = grad_weight(tokens, key_tok_grad) + grad_weight(memory_back, key_mem_grad)
    grad_value = grad_weight(tokens, value_tok_grad) + grad_weight(memory_back, value_mem_grad)
    grad_value_bias = column_sum(value_tok_grad) + column_sum(value_mem_grad)
    grad_memory = grad_input(key_mem_grad, key_back) + grad_input(value_mem_grad, value_back)
    grad_tokens = grad_first_sum + grad_input(query_grad, query_back)
    grad_tokens = (
        grad_tokens + grad_input(key_tok_grad, key_back) + grad_input(value_tok_grad, value_back)
    )
    owned = (
        lax.psum_scatter(grad_memory, "dp", scatter_dimension=1, tiled=True),
        lax.psum_scatter(grad_query, "dp", scatter_dimension=0, tiled=True),
        lax.psum_scatter(grad_query_bias, "dp", scatter_dimension=0, tiled=True),
        lax.psum_scatter(grad_key, "dp", scatter_dimension=0, tiled=True),
        lax.psum_scatter(grad_value, "dp", scatter_dimension=0, tiled=True),
        lax.psum_scatter(grad_value_bias, "dp", scatter_dimension=0, tiled=True),
        lax.psum_scatter(grad_out, "dp", scatter_dimension=0, tiled=True),
        lax.psum_scatter(grad_out_bias, "dp", scatter_dimension=0, tiled=True),
        lax.psum_scatter(grad_gain_one, "dp", scatter_dimension=0, tiled=True),
        lax.psum_scatter(grad_shift_one, "dp", scatter_dimension=0, tiled=True),
        lax.psum_scatter(grad_up, "dp", scatter_dimension=0, tiled=True),
        lax.psum_scatter(grad_up_bias, "dp", scatter_dimension=0, tiled=True),
        lax.psum_scatter(grad_down, "dp", scatter_dimension=0, tiled=True),
        lax.psum_scatter(grad_down_bias, "dp", scatter_dimension=0, tiled=True),
        lax.psum_scatter(grad_gain_two, "dp", scatter_dimension=0, tiled=True),
        lax.psum_scatter(grad_shift_two, "dp", scatter_dimension=0, tiled=True),
    )
    return (
        output,
        grad_tokens,
        owned[0],
        owned[1],
        owned[2],
        owned[3],
        owned[4],
        owned[5],
        owned[6],
        owned[7],
        owned[8],
        owned[9],
        owned[10],
        owned[11],
        owned[12],
        owned[13],
        owned[14],
        owned[15],
    )


def solution(mesh):
    in_specs = (
        P("dp", None),
        P("dp"),
        P("dp"),
        P(None, "dp"),
        P("dp", None),
        P("dp"),
        P("dp", None),
        P("dp", None),
        P("dp"),
        P("dp", None),
        P("dp"),
        P("dp"),
        P("dp"),
        P("dp", None),
        P("dp"),
        P("dp", None),
        P("dp"),
        P("dp"),
        P("dp"),
        P("dp", None),
    )
    out_specs = (
        P("dp", None),
        P("dp", None),
        P(None, "dp"),
        P("dp", None),
        P("dp"),
        P("dp", None),
        P("dp", None),
        P("dp"),
        P("dp", None),
        P("dp"),
        P("dp"),
        P("dp"),
        P("dp", None),
        P("dp"),
        P("dp", None),
        P("dp"),
        P("dp"),
        P("dp"),
    )
    return jax.shard_map(shards, mesh=mesh, in_specs=in_specs, out_specs=out_specs, check_vma=False)
```

profile of v0, /device:TPU:0, one launch (start us, length us, event | category | flops | bytes accessed | tf_op | source)
XLA Modules:
  0.0 2035.3 jit_solution(17654876365592954387)
XLA Ops:
  16.4 42.2 %all-reduce.19 = (bf16[512]{0:T(512)(128)(2,1)S(1)}, bf16[512]{0:T(512)(128)(2,1)S(1)}, bf16[512]{0:T(512)(128)(2,1)S(1)}, bf16[512]{0:T(512)(128)(2,1)S(1)}, bf...) all-reduce(bf16[512]{0:T(512)(128)(2,1)S(1)} %dynamic-update-slice,, ...), channel_id=1, replica_groups=mesh['dp'=32] {'dp'}, use_global_device_ids=true, to_apply=%add | all-reduce | flops 6144 | bytes 24576
  58.6 41.0 %all_gather.60 = bf16[20,512]{0,1:T(8,128)(2,1)S(1)} all-gather(bf16[20,16]{0,1:T(8,128)(2,1)} %param.27), channel_id=1, replica_groups=mesh['dp'=32] {'dp'}, dimensions={1}, use_global_device_ids=true | all-gather | bytes 21120 | tf_op jit(solution)/shard_map/all_gather | solution.py:67
  99.6 38.9 %all_gather.59 = bf16[512,512]{1,0:T(8,128)(2,1)S(1)} all-gather(bf16[16,512]{1,0:T(8,128)(2,1)} %param.30), channel_id=1, replica_groups=mesh['dp'=32] {'dp'}, dimensions={0}, use_global_device_ids=true | all-gather | bytes 540672 | tf_op jit(solution)/shard_map/all_gather | solution.py:70
  138.5 39.5 %all_gather.61 = bf16[512,512]{1,0:T(8,128)(2,1)S(1)} all-gather(bf16[16,512]{1,0:T(8,128)(2,1)} %param.31), channel_id=1, replica_groups=mesh['dp'=32] {'dp'}, dimensions={0}, use_global_device_ids=true | all-gather | bytes 540672 | tf_op jit(solution)/shard_map/all_gather | solution.py:71
  196.1 38.2 %all_gather.57 = bf16[512,512]{1,0:T(8,128)(2,1)S(1)} all-gather(bf16[16,512]{1,0:T(8,128)(2,1)S(1)} %copy-done.48), channel_id=1, replica_groups=mesh['dp'=32] {'dp'}, dimensions={0}, use_global_device_ids=true | all-gather | bytes 540672 | tf_op jit(solution)/shard_map/all_gather | solution.py:68
  234.3 42.2 %all_gather.63 = bf16[512,512]{1,0:T(8,128)(2,1)} all-gather(bf16[16,512]{1,0:T(8,128)(2,1)S(1)} %copy-done.49), channel_id=1, replica_groups=mesh['dp'=32] {'dp'}, dimensions={0}, use_global_device_ids=true | all-gather | bytes 540672 | tf_op jit(solution)/shard_map/all_gather | solution.py:73
  284.6 6.1 reshape.285
  290.7 5.4 copy.82
  297.7 208.1 %while.31 = (s32[]{:T(128)}, bf16[4,512,8,64]{1,3,2,0:T(8,128)(2,1)}, f32[4,8,512]{2,1,0:T(8,128)}, s32[2048]{0:T(1024)}, s32[4,512]{1,0:T(4,128)}, /*index=5*/b...) while((s32[]{:T(128)}, ...), condition=%wide.region_5.6_spmd, body=%wide.region_0.5_spmd.sunk | while | flops 2271260672 | bytes 114112640 | solution.py:156
  301.0 14.8 fusion.188
  315.9 15.0 fusion.190
  331.5 15.7 fusion.192
  352.9 14.8 fusion.188
  367.8 15.0 fusion.190
  383.4 15.7 fusion.192
  404.8 14.8 fusion.188
  419.7 15.0 fusion.190
  435.3 15.7 fusion.192
  456.8 14.8 fusion.188
  471.6 15.0 fusion.190
  487.2 15.7 fusion.192
  515.2 46.5 %multiply_convert_fusion.2 = (bf16[2048,2048]{1,0:T(8,128)(2,1)}, f32[2048,2048]{1,0:T(8,128)}, f32[2048,2048]{1,0:T(8,128)}) fusion(f32[2048]{0:T(1024)S(1)} %copy-done.56, bf16[512,2048]{1,0:T(8,128)(2,1)} %all-gather.3.cloned.1.call-done, f32[2048,512]{0,1:T(8,128)} %copy-done.10, f32[512]{0:T(512)S(1)} %copy-done.61, f32[512]{0:T(512)S(1)} %copy-done.57, ...), kind=kOutput, calls=%fused_computation.84 | convolution fusion | flops 4577034240 | bytes 48263168 | tf_op jit(solution)/shard_map/dot_general | solution.py:25
  561.9 11.1 fusion.81
  577.7 4.8 convert_reduce_fusion.1
  582.5 22.8 %convert_reduce_fusion = (f32[2048]{0:T(1024)}, bf16[2048,2048]{1,0:T(8,128)(2,1)}) fusion(f32[2048,2048]{1,0:T(8,128)} %get-tuple-element.425, bf16[2048,512]{0,1:T(8,128)(2,1)} %get-tuple-element.415, bf16[2048,512]{1,0:T(8,128)(2,1)} %all-gather.5.cloned.1.call-done, f32[2048,2048]{1,0:T(8,128)} %get-tuple-element.439, f32[2048]{0:T(1024)S(1)} %copy-done.56), kind=kOutput, calls=%fused_computation.82 | convolution fusion | flops 4366268416 | bytes 46153728 | tf_op jit(solution)/shard_map/dot_general | solution.py:35
  605.2 12.9 multiply_reduce_fusion.3
  629.0 5.6 copy.90
  636.2 445.1 %while.32 = (s32[]{:T(128)}, f32[2048,8,64]{0,2,1:T(8,128)}, f32[2048,8,64]{0,2,1:T(8,128)}, f32[20,8,64]{2,0,1:T(8,128)S(1)}, f32[20,8,64]{2,0,1:T(8,128)S(1)},...) while((s32[]{:T(128)}, f32[2048,8,64]{0,2,1:T(8,128)}, ...), condition=%wide.region_17.18_spmd.clone, body=%wide.region_14.17_spmd.clone.sunk | while | flops 5504415744 | bytes 366266624 | solution.py:269
  643.2 14.1 fusion.212
  657.4 24.6 %multiply_reduce_fusion.10 = (f32[8,512]{1,0:T(8,128)S(1)}, f32[8,512,2048]{2,1,0:T(8,128)}) fusion(f32[8,512,2048]{2,1,0:T(8,128)} %fusion.212, f32[8,512]{1,0:T(8,128)S(1)} %dynamic-slice_bitcast_fusion.2, bf16[2048,8,64]{0,2,1:T(8,128)(2,1)S(1)} %get-tuple-element.693, bf16[4,512,8,64]{1,3,2,0:T(8,128)(2,1)} %get-tuple-element.690, ...), kind=kOutput, calls=%fused_computation.29.clone.1 | convolution fusion | flops 1115680768 | bytes 70811648 | tf_op jit(solution)/shard_map/while/body/eval_jaxpr/qhd,khd->hqk/dot_general | solution.py:127
  682.0 27.4 %multiply_convert_fusion.5 = bf16[8,512,2048]{2,1,0:T(8,128)(2,1)} fusion(f32[8,512,2048]{2,1,0:T(8,128)} %get-tuple-element.613, f32[8,512,2048]{2,1,0:T(8,128)} %fusion.212, f32[8,512]{1,0:T(8,128)S(1)} %add.399), kind=kLoop, calls=%fused_computation.28.clone.1 | loop fusion | flops 25165824 | bytes 83902464 | tf_op jit(solution)/shard_map/while/body/eval_jaxpr/convert_element_type | solution.py:225
  709.4 15.7 bitcast_add_fusion.5
  726.5 9.8 fusion.216
  737.5 6.3 bitcast_add_fusion.4
  752.5 14.2 fusion.212
  766.7 24.7 %multiply_reduce_fusion.10 = (f32[8,512]{1,0:T(8,128)S(1)}, f32[8,512,2048]{2,1,0:T(8,128)}) fusion(f32[8,512,2048]{2,1,0:T(8,128)} %fusion.212, f32[8,512]{1,0:T(8,128)S(1)} %dynamic-slice_bitcast_fusion.2, bf16[2048,8,64]{0,2,1:T(8,128)(2,1)S(1)} %get-tuple-element.693, bf16[4,512,8,64]{1,3,2,0:T(8,128)(2,1)} %get-tuple-element.690, ...), kind=kOutput, calls=%fused_computation.29.clone.1 | convolution fusion | flops 1115680768 | bytes 70811648 | tf_op jit(solution)/shard_map/while/body/eval_jaxpr/qhd,khd->hqk/dot_general | solution.py:127
  791.3 27.4 %multiply_convert_fusion.5 = bf16[8,512,2048]{2,1,0:T(8,128)(2,1)} fusion(f32[8,512,2048]{2,1,0:T(8,128)} %get-tuple-element.613, f32[8,512,2048]{2,1,0:T(8,128)} %fusion.212, f32[8,512]{1,0:T(8,128)S(1)} %add.399), kind=kLoop, calls=%fused_computation.28.clone.1 | loop fusion | flops 25165824 | bytes 83902464 | tf_op jit(solution)/shard_map/while/body/eval_jaxpr/convert_element_type | solution.py:225
  818.7 16.9 bitcast_add_fusion.5
  837.0 9.8 fusion.216
  847.9 7.6 bitcast_add_fusion.4
  864.3 14.2 fusion.212
  878.5 24.6 %multiply_reduce_fusion.10 = (f32[8,512]{1,0:T(8,128)S(1)}, f32[8,512,2048]{2,1,0:T(8,128)}) fusion(f32[8,512,2048]{2,1,0:T(8,128)} %fusion.212, f32[8,512]{1,0:T(8,128)S(1)} %dynamic-slice_bitcast_fusion.2, bf16[2048,8,64]{0,2,1:T(8,128)(2,1)S(1)} %get-tuple-element.693, bf16[4,512,8,64]{1,3,2,0:T(8,128)(2,1)} %get-tuple-element.690, ...), kind=kOutput, calls=%fused_computation.29.clone.1 | convolution fusion | flops 1115680768 | bytes 70811648 | tf_op jit(solution)/shard_map/while/body/eval_jaxpr/qhd,khd->hqk/dot_general | solution.py:127
  903.1 27.4 %multiply_convert_fusion.5 = bf16[8,512,2048]{2,1,0:T(8,128)(2,1)} fusion(f32[8,512,2048]{2,1,0:T(8,128)} %get-tuple-element.613, f32[8,512,2048]{2,1,0:T(8,128)} %fusion.212, f32[8,512]{1,0:T(8,128)S(1)} %add.399), kind=kLoop, calls=%fused_computation.28.clone.1 | loop fusion | flops 25165824 | bytes 83902464 | tf_op jit(solution)/shard_map/while/body/eval_jaxpr/convert_element_type | solution.py:225
  930.5 16.9 bitcast_add_fusion.5
  948.8 9.8 fusion.216
  959.7 7.6 bitcast_add_fusion.4
  976.1 14.1 fusion.212
  990.3 24.6 %multiply_reduce_fusion.10 = (f32[8,512]{1,0:T(8,128)S(1)}, f32[8,512,2048]{2,1,0:T(8,128)}) fusion(f32[8,512,2048]{2,1,0:T(8,128)} %fusion.212, f32[8,512]{1,0:T(8,128)S(1)} %dynamic-slice_bitcast_fusion.2, bf16[2048,8,64]{0,2,1:T(8,128)(2,1)S(1)} %get-tuple-element.693, bf16[4,512,8,64]{1,3,2,0:T(8,128)(2,1)} %get-tuple-element.690, ...), kind=kOutput, calls=%fused_computation.29.clone.1 | convolution fusion | flops 1115680768 | bytes 70811648 | tf_op jit(solution)/shard_map/while/body/eval_jaxpr/qhd,khd->hqk/dot_general | solution.py:127
  1014.9 27.4 %multiply_convert_fusion.5 = bf16[8,512,2048]{2,1,0:T(8,128)(2,1)} fusion(f32[8,512,2048]{2,1,0:T(8,128)} %get-tuple-element.613, f32[8,512,2048]{2,1,0:T(8,128)} %fusion.212, f32[8,512]{1,0:T(8,128)S(1)} %add.399), kind=kLoop, calls=%fused_computation.28.clone.1 | loop fusion | flops 25165824 | bytes 83902464 | tf_op jit(solution)/shard_map/while/body/eval_jaxpr/convert_element_type | solution.py:225
  1042.3 16.9 bitcast_add_fusion.5
  1060.6 9.8 fusion.216
  1071.5 7.6 bitcast_add_fusion.4
  1085.0 4.6 fusion.86
  1110.0 11.2 fusion.72
  1121.5 10.5 fusion.87
  1146.1 5.3 copy.100
  1151.5 37.4 %all-reduce.18 = (f32[512]{0:T(512)S(1)}, f32[512]{0:T(512)S(1)}, f32[512]{0:T(512)S(1)}, f32[512]{0:T(512)S(1)}, f32[512]{0:T(512)S(1)}, /*index=5*/f32[2048]{0...) all-reduce(f32[512]{0:T(512)S(1)} %reduce_sum.215, ...), channel_id=4, replica_groups=mesh['dp'=32] {'dp'}, use_global_device_ids=true, to_apply=%region_21.22.clone | all-reduce | flops 6144 | bytes 49152
  1194.1 20.8 %reduce-scatter.14.cloned.1.call-done = f32[20,16]{0,1:T(8,128)} async-done(((f32[20,512]{0,1:T(8,128)}), f32[20,16]{0,1:T(8,128)}) %reduce-scatter.14.cloned.1.call-update) | async-done | bytes 1296 | tf_op jit(solution)/shard_map/reduce_scatter | solution.py:288
  1214.9 133.5 %reduce-scatter.16.cloned.1.call-done = f32[16,512]{1,0:T(8,128)} async-done(((f32[512,512]{1,0:T(8,128)}), f32[16,512]{1,0:T(8,128)}) %reduce-scatter.16.cloned.1.call-update) | async-done | bytes 32784 | tf_op jit(solution)/shard_map/reduce_scatter | solution.py:294
  1348.3 133.4 %reduce-scatter.22.cloned.1.call-done = f32[16,512]{1,0:T(8,128)} async-done(((f32[512,512]{1,0:T(8,128)}), f32[16,512]{1,0:T(8,128)}) %reduce-scatter.22.cloned.1.call-update) | async-done | bytes 32784
  1481.8 133.5 %reduce-scatter.24.cloned.1.call-done = f32[16,512]{1,0:T(8,128)} async-done(((f32[512,512]{1,0:T(8,128)}), f32[16,512]{1,0:T(8,128)}) %reduce-scatter.24.cloned.1.call-update) | async-done | bytes 32784
  1615.3 133.6 %reduce-scatter.26.cloned.1.call-done = f32[16,512]{1,0:T(8,128)} async-done(((f32[512,512]{1,0:T(8,128)}), f32[16,512]{1,0:T(8,128)}) %reduce-scatter.26.cloned.1.call-update) | async-done | bytes 32784
  1748.8 139.7 %reduce-scatter.18.cloned.1.call-done = f32[16,2048]{1,0:T(8,128)} async-done(((f32[512,2048]{1,0:T(8,128)}), f32[16,2048]{1,0:T(8,128)}) %reduce-scatter.18.cloned.1.call-update) | async-done | bytes 131088 | tf_op jit(solution)/shard_map/reduce_scatter | solution.py:298
  1888.5 139.8 %reduce-scatter.20.cloned.1.call-done = f32[64,512]{1,0:T(8,128)} async-done(((f32[2048,512]{1,0:T(8,128)}), f32[64,512]{1,0:T(8,128)}) %reduce-scatter.20.cloned.1.call-update) | async-done | bytes 131088 | tf_op jit(solution)/shard_map/reduce_scatter | solution.py:300
  (338 shorter events, 176.2 us)
Async XLA Ops:
  7.2 508.0 %all-gather.3.cloned.1.call-start = ((), (), s32[]{:S(2)}) async-start(), calls=%async_computation.7 | async-start | bytes 2162688 | tf_op jit(solution)/shard_map/all_gather | solution.py:77
  7.9 553.9 %all-gather.5.cloned.1.call-start = ((), (), s32[]{:S(2)}) async-start(), calls=%async_computation.8 | async-start | bytes 2162688 | tf_op jit(solution)/shard_map/all_gather | solution.py:79
  8.7 1206.2 %reduce-scatter.14.cloned.1.call-start = ((), (), s32[]{:S(2)}) async-start(), calls=%async_computation.9 | async-start | bytes 270336 | tf_op jit(solution)/shard_map/reduce_scatter | solution.py:288
  99.6 78.6 %copy-start.23 = (bf16[20,512]{0,1:T(8,128)(2,1)}, bf16[20,512]{0,1:T(8,128)(2,1)S(1)}, u32[]{:S(2)}) copy-start(bf16[20,512]{0,1:T(8,128)(2,1)S(1)} %all_gather.60) | copy-start | bytes 61444
  138.5 44.3 %copy-start.19 = (bf16[512,512]{1,0:T(8,128)(2,1)}, bf16[512,512]{1,0:T(8,128)(2,1)S(1)}, u32[]{:S(2)}) copy-start(bf16[512,512]{1,0:T(8,128)(2,1)S(1)} %all_gather.59) | copy-start | bytes 1572868
  178.0 4.8 copy-start.13
  178.2 4.6 copy-start.26
  184.1 9.3 copy-start.45
  184.1 12.0 copy-start.48
  184.1 50.1 %copy-start.49 = (bf16[16,512]{1,0:T(8,128)(2,1)S(1)}, bf16[16,512]{1,0:T(8,128)(2,1)}, u32[]{:S(2)}) copy-start(bf16[16,512]{1,0:T(8,128)(2,1)} %param.33) | copy-start | bytes 49156
  234.3 50.3 %copy-start.32 = (bf16[512,512]{1,0:T(8,128)(2,1)}, bf16[512,512]{1,0:T(8,128)(2,1)S(1)}, u32[]{:S(2)}) copy-start(bf16[512,512]{1,0:T(8,128)(2,1)S(1)} %all_gather.57) | copy-start | bytes 1572868
  505.7 4.7 copy-start.1
  505.8 4.7 copy-start.31
  505.8 4.7 copy-start.35
  505.8 4.7 copy-start.64
  512.0 3.2 copy-start.56
  512.1 3.2 copy-start.57
  512.1 3.2 copy-start.61
  512.1 106.1 %copy-start.41 = (f32[2048]{0:T(1024)}, f32[2048]{0:T(1024)S(1)}, u32[]{:S(2)}) copy-start(f32[2048]{0:T(1024)S(1)} %broadcast_multiply_fusion.1) | copy-start | bytes 24580
  515.2 103.0 %copy-start.46 = (f32[2048]{0:T(1024)}, f32[2048]{0:T(1024)S(1)}, u32[]{:S(2)}) copy-start(f32[2048]{0:T(1024)S(1)} %fusion.70) | copy-start | bytes 24580
  515.2 46.6 %copy-start.63 = (f32[512]{0:T(512)S(1)}, f32[512]{0:T(512)}, u32[]{:S(2)}) copy-start(f32[512]{0:T(512)} %convert_element_type.163) | copy-start | bytes 6148
  561.8 11.2 copy-start.8
  561.8 11.2 copy-start.43
  561.8 11.2 copy-start.44
  573.0 4.7 copy-start.5
  605.2 12.9 copy-start.40
  605.2 13.0 copy-start.11
  619.7 4.3 copy-start.36
  629.0 7.2 copy-start.2
  629.0 7.2 copy-start.21
  629.0 7.2 copy-start.22
  629.0 7.2 copy-start.34
  636.4 6.8 copy-start.4
  726.5 10.9 copy-start
  737.5 6.3 copy-start.3
  745.7 6.8 copy-start.4
  837.0 10.9 copy-start
  847.9 7.6 copy-start.3
  857.5 6.8 copy-start.4
  948.8 10.9 copy-start
  959.7 7.6 copy-start.3
  969.3 6.8 copy-start.4
  1060.6 10.9 copy-start
  1071.5 7.6 copy-start.3
  1085.0 4.7 copy-start.9
  1085.0 263.4 %reduce-scatter.16.cloned.1.call-start = ((), (), s32[]{:S(2)}) async-start(), calls=%async_computation.10 | async-start | bytes 1081344 | tf_op jit(solution)/shard_map/reduce_scatter | solution.py:294
  1089.7 392.1 %reduce-scatter.22.cloned.1.call-start = ((), (), s32[]{:S(2)}) async-start(), calls=%async_computation.13 | async-start | bytes 1081344
  1089.7 3.7 copy-start.27
  1096.0 519.3 %reduce-scatter.24.cloned.1.call-start = ((), (), s32[]{:S(2)}) async-start(), calls=%async_computation.14 | async-start | bytes 1081344
  1096.0 4.0 copy-start.28
  1102.9 645.9 %reduce-scatter.26.cloned.1.call-start = ((), (), s32[]{:S(2)}) async-start(), calls=%async_computation.15 | async-start | bytes 1081344
  1103.0 4.0 copy-start.29
  1109.9 778.6 %reduce-scatter.18.cloned.1.call-start = ((), (), s32[]{:S(2)}) async-start(), calls=%async_computation.11 | async-start | bytes 4325376 | tf_op jit(solution)/shard_map/reduce_scatter | solution.py:298
  1121.2 907.0 %reduce-scatter.20.cloned.1.call-start = ((), (), s32[]{:S(2)}) async-start(), calls=%async_computation.12 | async-start | bytes 4325376 | tf_op jit(solution)/shard_map/reduce_scatter | solution.py:300
  1132.1 4.5 copy-start.20
  1136.1 3.5 copy-start.33
  1136.6 4.3 copy-start.38
  1146.0 5.4 copy-start.50
  1146.0 5.4 copy-start.51
  1146.0 5.4 copy-start.52
  1146.0 5.4 copy-start.53
  1146.0 5.4 copy-start.55
  1146.0 5.4 copy-start.59
  1146.1 5.4 copy-start.60
  (19 other events, 37.3 us)
Sparse Core Ops, SparseCore 0:
  10.9 59.0 all-gather.2
  72.9 55.6 all-gather.4
  1085.1 129.7 reduce-scatter.13
  1217.6 130.6 reduce-scatter.15
  1351.0 130.7 reduce-scatter.21
  1484.5 130.6 reduce-scatter.23
  1618.1 130.7 reduce-scatter.25
  1751.8 136.6 reduce-scatter.17
  1891.5 136.7 reduce-scatter.19
where the time goes:
time: 2040 us
  waiting for transfers between devices  836 us (41%)
  matrix products  603 us (30%)
  blocking collectives  279 us (14%)
  other arithmetic  207 us (10%)
  local copies, waits for them, and re-layouts  92.5 us (5%)
    unnamed x12, waiting for transfers between devices  402 us
    dot_general x8, matrix products, score_block(): jnp.einsum('qhd,khd->hqk', query_block, key_heads, preferred_element_type...  158 us
    reduce_scatter x1, waiting for transfers between devices, shards(): lax.psum_scatter(grad_down, 'dp', scatter_dimension=0, tiled=True)  140 us
    reduce_scatter x1, waiting for transfers between devices, shards(): lax.psum_scatter(grad_up, 'dp', scatter_dimension=0, tiled=True)  140 us
    reduce_scatter x1, waiting for transfers between devices, shards(): lax.psum_scatter(grad_out, 'dp', scatter_dimension=0, tiled=True)  133 us
    convert_element_type x4, other arithmetic, backward_block(): (tok_probs * (tok_dprobs - centre[..., None])).astype(jnp.bfloat16)  110 us
    unnamed x2, blocking collectives  79.6 us
    dot_general x8, matrix products, matmul(): return jnp.dot(left, right, preferred_element_type=jnp.float32)  69.4 us
  transfers between devices with their start and end apart: 9, of which 7 were waited for; matrix products, arithmetic and copies ran while one was open for 18% of the time, Pallas kernels for 0%

commit v1 on v0

--- a/solution.py
+++ b/solution.py
@@ -8,6 +8,28 @@
 QB = 512
 EPS = 1e-05
 NEG = -1e30
+
+
+def in_order(blocks, dim):
+    dims = list(blocks.shape[1:])
+    dims[dim] *= blocks.shape[0]
+    return jnp.moveaxis(blocks, 0, dim).reshape(dims)
+
+
+def doubled(x, axis):
+    size = lax.axis_size(axis)
+    blocks = x[None]
+    for level in range(size.bit_length() - 1):
+        distance = 1 << level
+        received = lax.ppermute(blocks, axis, [(i, i ^ distance) for i in range(size)])
+        both = jnp.stack([blocks, received])
+        upper = lax.axis_index(axis) >> level & 1
+        blocks = jnp.where(upper == 0, both, both[::-1]).reshape(-1, *x.shape)
+    return blocks
+
+
+def gather_by_bits(shard, axis, dim):
+    return in_order(doubled(shard, axis), dim)
 
 
 def normalize(value, gain):
@@ -70,7 +92,7 @@
         lax.all_gather(w_key, "dp", axis=0, tiled=True),
         lax.all_gather(w_value, "dp", axis=0, tiled=True),
         lax.all_gather(b_value, "dp", axis=0, tiled=True),
-        lax.all_gather(w_out, "dp", axis=0, tiled=True),
+        gather_by_bits(w_out, "dp", 0),
         lax.all_gather(b_out, "dp", axis=0, tiled=True),
         lax.all_gather(gain_attn, "dp", axis=0, tiled=True),
         lax.all_gather(shift_attn, "dp", axis=0, tiled=True),

time: 2040 us -> 2050 us (level)
    unnamed x161 -> x169, local copies, waits for them, and re-layouts: 52.6 us -> 53.1 us
  transfers between devices with their start and end apart: 9 -> 14, of which waited for: 7 -> 8; matrix products, arithmetic and copies ran while one was open for 18% -> 18% of each run, Pallas kernels for 0% -> 0%
where the time goes in v1:
time: 2050 us; the launch traced here: 2040 us
  waiting for transfers between devices  836 us (41%)
  matrix products  602 us (29%)
  blocking collectives  284 us (14%)
  other arithmetic  207 us (10%)
  local copies, waits for them, and re-layouts  92.2 us (4%)
    unnamed x12, waiting for transfers between devices  401 us
    dot_general x8, matrix products, score_block(): jnp.einsum('qhd,khd->hqk', query_block, key_heads, preferred_element_type...  158 us
    reduce_scatter x1, waiting for transfers between devices, shards(): lax.psum_scatter(grad_up, 'dp', scatter_dimension=0, tiled=True)  140 us
    reduce_scatter x1, waiting for transfers between devices, shards(): lax.psum_scatter(grad_down, 'dp', scatter_dimension=0, tiled=True)  140 us
    reduce_scatter x1, waiting for transfers between devices, shards(): lax.psum_scatter(grad_out, 'dp', scatter_dimension=0, tiled=True)  134 us
    convert_element_type x4, other arithmetic, backward_block(): (tok_probs * (tok_dprobs - centre[..., None])).astype(jnp.bfloat16)  110 us
    unnamed x2, blocking collectives  79.6 us
    dot_general x8, matrix products, matmul(): return jnp.dot(left, right, preferred_element_type=jnp.float32)  68 us
  transfers between devices with their start and end apart: 14, of which 8 were waited for; matrix products, arithmetic and copies ran while one was open for 18% of the time, Pallas kernels for 0%

profile of v1, /device:TPU:0, one launch (start us, length us, event | category | flops | bytes accessed | tf_op | source)
XLA Modules:
  0.0 2042.5 jit_solution(321302888856562831)
XLA Ops:
  16.4 42.2 %all-reduce.19 = (bf16[512]{0:T(512)(128)(2,1)S(1)}, bf16[512]{0:T(512)(128)(2,1)S(1)}, bf16[512]{0:T(512)(128)(2,1)}, bf16[512]{0:T(512)(128)(2,1)}, bf16[512]{...) all-reduce(bf16[512]{0:T(512)(128)(2,1)S(1)} %dynamic-update-slice,, ...), channel_id=1, replica_groups=mesh['dp'=32] {'dp'}, use_global_device_ids=true, to_apply=%add | all-reduce | flops 6144 | bytes 24576
  58.6 41.4 %all_gather.59 = bf16[20,512]{0,1:T(8,128)(2,1)S(1)} all-gather(bf16[20,16]{0,1:T(8,128)(2,1)} %param.27), channel_id=1, replica_groups=mesh['dp'=32] {'dp'}, dimensions={1}, use_global_device_ids=true | all-gather | bytes 21120 | tf_op jit(solution)/shard_map/all_gather | solution.py:89
  100.0 38.8 %all_gather.58 = bf16[512,512]{1,0:T(8,128)(2,1)S(1)} all-gather(bf16[16,512]{1,0:T(8,128)(2,1)} %param.30), channel_id=1, replica_groups=mesh['dp'=32] {'dp'}, dimensions={0}, use_global_device_ids=true | all-gather | bytes 540672 | tf_op jit(solution)/shard_map/all_gather | solution.py:92
  138.8 39.7 %all_gather.60 = bf16[512,512]{1,0:T(8,128)(2,1)S(1)} all-gather(bf16[16,512]{1,0:T(8,128)(2,1)} %param.31), channel_id=1, replica_groups=mesh['dp'=32] {'dp'}, dimensions={0}, use_global_device_ids=true | all-gather | bytes 540672 | tf_op jit(solution)/shard_map/all_gather | solution.py:93
  178.5 38.3 %all_gather.56 = bf16[512,512]{1,0:T(8,128)(2,1)S(1)} all-gather(bf16[16,512]{1,0:T(8,128)(2,1)} %param.28), channel_id=1, replica_groups=mesh['dp'=32] {'dp'}, dimensions={0}, use_global_device_ids=true | all-gather | bytes 540672 | tf_op jit(solution)/shard_map/all_gather | solution.py:90
  232.3 6.3 reshape.301
  238.6 5.4 copy.82
  246.3 207.4 %while.31 = (s32[]{:T(128)}, bf16[4,512,8,64]{1,3,2,0:T(8,128)(2,1)}, f32[4,8,512]{2,1,0:T(8,128)}, s32[2048]{0:T(1024)}, s32[4,512]{1,0:T(4,128)}, /*index=5*/b...) while((s32[]{:T(128)}, ...), condition=%wide.region_5.6_spmd, body=%wide.region_0.5_spmd.sunk | while | flops 2271260672 | bytes 114112640 | solution.py:178
  249.6 14.7 fusion.190
  264.4 15.0 fusion.192
  280.1 15.7 fusion.194
  301.5 14.7 fusion.190
  316.3 15.0 fusion.192
  331.9 15.7 fusion.194
  353.3 14.7 fusion.190
  368.2 15.0 fusion.192
  383.8 15.7 fusion.194
  405.2 14.7 fusion.190
  420.0 15.0 fusion.192
  435.6 15.7 fusion.194
  471.2 46.0 %all_gather.71 = bf16[512,512]{1,0:T(8,128)(2,1)} all-gather(bf16[16,512]{1,0:T(8,128)(2,1)S(1)} %copy-done.43), channel_id=1, replica_groups=mesh['dp'=32] {'dp'}, dimensions={0}, use_global_device_ids=true | all-gather | bytes 540672 | tf_op jit(solution)/shard_map/all_gather | solution.py:195
  522.1 46.5 %multiply_convert_fusion.2 = (bf16[2048,2048]{1,0:T(8,128)(2,1)}, f32[2048,2048]{1,0:T(8,128)}, f32[2048,2048]{1,0:T(8,128)}) fusion(f32[2048]{0:T(1024)S(1)} %convert_element_type.161, bf16[512,2048]{1,0:T(8,128)(2,1)} %all-gather.3.cloned.1.call-done, f32[2048,512]{0,1:T(8,128)} %copy-done.10, f32[512]{0:T(512)S(1)} %convert_element_type.159, ...), kind=kOutput, calls=%fused_computation.84 | convolution fusion | flops 4577034240 | bytes 48263168 | tf_op jit(solution)/shard_map/dot_general | solution.py:47
  568.7 11.1 fusion.83
  584.5 4.8 convert_reduce_fusion.1
  589.3 22.8 %convert_reduce_fusion = (f32[2048]{0:T(1024)}, bf16[2048,2048]{1,0:T(8,128)(2,1)}) fusion(f32[2048,2048]{1,0:T(8,128)} %get-tuple-element.425, bf16[2048,512]{0,1:T(8,128)(2,1)} %get-tuple-element.415, bf16[2048,512]{1,0:T(8,128)(2,1)} %all-gather.5.cloned.1.call-done, f32[2048,2048]{1,0:T(8,128)} %get-tuple-element.441, f32[2048]{0:T(1024)S(1)} %convert_element_type.161), kind=kOutput, calls=%fused_computation.82 | convolution fusion | flops 4366268416 | bytes 46153728 | tf_op jit(solution)/shard_map/dot_general | solution.py:57
  612.0 12.9 multiply_reduce_fusion.3
  635.8 5.6 copy.90
  643.0 445.6 %while.32 = (s32[]{:T(128)}, f32[2048,8,64]{0,2,1:T(8,128)}, f32[2048,8,64]{0,2,1:T(8,128)}, f32[20,8,64]{2,0,1:T(8,128)S(1)}, f32[20,8,64]{2,0,1:T(8,128)S(1)},...) while((s32[]{:T(128)}, f32[2048,8,64]{0,2,1:T(8,128)}, ...), condition=%wide.region_17.18_spmd.clone, body=%wide.region_14.17_spmd.clone.sunk | while | flops 5504415744 | bytes 366266624 | solution.py:291
  650.0 14.2 fusion.214
  664.2 24.7 %multiply_reduce_fusion.10 = (f32[8,512]{1,0:T(8,128)S(1)}, f32[8,512,2048]{2,1,0:T(8,128)}) fusion(f32[8,512,2048]{2,1,0:T(8,128)} %fusion.214, f32[8,512]{1,0:T(8,128)S(1)} %dynamic-slice_bitcast_fusion.2, bf16[2048,8,64]{0,2,1:T(8,128)(2,1)S(1)} %get-tuple-element.695, bf16[4,512,8,64]{1,3,2,0:T(8,128)(2,1)} %get-tuple-element.692, ...), kind=kOutput, calls=%fused_computation.29.clone.1 | convolution fusion | flops 1115680768 | bytes 70811648 | tf_op jit(solution)/shard_map/while/body/eval_jaxpr/qhd,khd->hqk/dot_general | solution.py:149
  688.9 27.5 %multiply_convert_fusion.5 = bf16[8,512,2048]{2,1,0:T(8,128)(2,1)} fusion(f32[8,512,2048]{2,1,0:T(8,128)} %get-tuple-element.615, f32[8,512,2048]{2,1,0:T(8,128)} %fusion.214, f32[8,512]{1,0:T(8,128)S(1)} %add.399), kind=kLoop, calls=%fused_computation.28.clone.1 | loop fusion | flops 25165824 | bytes 83902464 | tf_op jit(solution)/shard_map/while/body/eval_jaxpr/convert_element_type | solution.py:247
  716.4 15.7 bitcast_add_fusion.5
  733.4 9.9 fusion.218
  744.4 6.3 bitcast_add_fusion.4
  759.4 14.2 fusion.214
  773.6 24.7 %multiply_reduce_fusion.10 = (f32[8,512]{1,0:T(8,128)S(1)}, f32[8,512,2048]{2,1,0:T(8,128)}) fusion(f32[8,512,2048]{2,1,0:T(8,128)} %fusion.214, f32[8,512]{1,0:T(8,128)S(1)} %dynamic-slice_bitcast_fusion.2, bf16[2048,8,64]{0,2,1:T(8,128)(2,1)S(1)} %get-tuple-element.695, bf16[4,512,8,64]{1,3,2,0:T(8,128)(2,1)} %get-tuple-element.692, ...), kind=kOutput, calls=%fused_computation.29.clone.1 | convolution fusion | flops 1115680768 | bytes 70811648 | tf_op jit(solution)/shard_map/while/body/eval_jaxpr/qhd,khd->hqk/dot_general | solution.py:149
  798.3 27.5 %multiply_convert_fusion.5 = bf16[8,512,2048]{2,1,0:T(8,128)(2,1)} fusion(f32[8,512,2048]{2,1,0:T(8,128)} %get-tuple-element.615, f32[8,512,2048]{2,1,0:T(8,128)} %fusion.214, f32[8,512]{1,0:T(8,128)S(1)} %add.399), kind=kLoop, calls=%fused_computation.28.clone.1 | loop fusion | flops 25165824 | bytes 83902464 | tf_op jit(solution)/shard_map/while/body/eval_jaxpr/convert_element_type | solution.py:247
  825.8 16.9 bitcast_add_fusion.5
  844.1 9.9 fusion.218
  855.0 7.6 bitcast_add_fusion.4
  871.4 14.2 fusion.214
  885.5 24.7 %multiply_reduce_fusion.10 = (f32[8,512]{1,0:T(8,128)S(1)}, f32[8,512,2048]{2,1,0:T(8,128)}) fusion(f32[8,512,2048]{2,1,0:T(8,128)} %fusion.214, f32[8,512]{1,0:T(8,128)S(1)} %dynamic-slice_bitcast_fusion.2, bf16[2048,8,64]{0,2,1:T(8,128)(2,1)S(1)} %get-tuple-element.695, bf16[4,512,8,64]{1,3,2,0:T(8,128)(2,1)} %get-tuple-element.692, ...), kind=kOutput, calls=%fused_computation.29.clone.1 | convolution fusion | flops 1115680768 | bytes 70811648 | tf_op jit(solution)/shard_map/while/body/eval_jaxpr/qhd,khd->hqk/dot_general | solution.py:149
  910.3 27.5 %multiply_convert_fusion.5 = bf16[8,512,2048]{2,1,0:T(8,128)(2,1)} fusion(f32[8,512,2048]{2,1,0:T(8,128)} %get-tuple-element.615, f32[8,512,2048]{2,1,0:T(8,128)} %fusion.214, f32[8,512]{1,0:T(8,128)S(1)} %add.399), kind=kLoop, calls=%fused_computation.28.clone.1 | loop fusion | flops 25165824 | bytes 83902464 | tf_op jit(solution)/shard_map/while/body/eval_jaxpr/convert_element_type | solution.py:247
  937.7 16.9 bitcast_add_fusion.5
  956.0 9.9 fusion.218
  966.9 7.6 bitcast_add_fusion.4
  983.3 14.2 fusion.214
  997.5 24.7 %multiply_reduce_fusion.10 = (f32[8,512]{1,0:T(8,128)S(1)}, f32[8,512,2048]{2,1,0:T(8,128)}) fusion(f32[8,512,2048]{2,1,0:T(8,128)} %fusion.214, f32[8,512]{1,0:T(8,128)S(1)} %dynamic-slice_bitcast_fusion.2, bf16[2048,8,64]{0,2,1:T(8,128)(2,1)S(1)} %get-tuple-element.695, bf16[4,512,8,64]{1,3,2,0:T(8,128)(2,1)} %get-tuple-element.692, ...), kind=kOutput, calls=%fused_computation.29.clone.1 | convolution fusion | flops 1115680768 | bytes 70811648 | tf_op jit(solution)/shard_map/while/body/eval_jaxpr/qhd,khd->hqk/dot_general | solution.py:149
  1022.2 27.5 %multiply_convert_fusion.5 = bf16[8,512,2048]{2,1,0:T(8,128)(2,1)} fusion(f32[8,512,2048]{2,1,0:T(8,128)} %get-tuple-element.615, f32[8,512,2048]{2,1,0:T(8,128)} %fusion.214, f32[8,512]{1,0:T(8,128)S(1)} %add.399), kind=kLoop, calls=%fused_computation.28.clone.1 | loop fusion | flops 25165824 | bytes 83902464 | tf_op jit(solution)/shard_map/while/body/eval_jaxpr/convert_element_type | solution.py:247
  1049.6 16.9 bitcast_add_fusion.5
  1067.9 9.9 fusion.218
  1078.8 7.6 bitcast_add_fusion.4
  1092.3 4.6 fusion.88
  1117.4 11.2 fusion.74
  1128.9 10.6 fusion.89
  1153.5 5.3 copy.100
  1158.9 37.3 %all-reduce.18 = (f32[512]{0:T(512)S(1)}, f32[512]{0:T(512)S(1)}, f32[512]{0:T(512)S(1)}, f32[512]{0:T(512)S(1)}, f32[512]{0:T(512)S(1)}, /*index=5*/f32[2048]{0...) all-reduce(f32[512]{0:T(512)S(1)} %reduce_sum.215, ...), channel_id=4, replica_groups=mesh['dp'=32] {'dp'}, use_global_device_ids=true, to_apply=%region_21.22.clone | all-reduce | flops 6144 | bytes 49152
  1201.4 20.6 %reduce-scatter.14.cloned.1.call-done = f32[20,16]{0,1:T(8,128)} async-done(((f32[20,512]{0,1:T(8,128)}), f32[20,16]{0,1:T(8,128)}) %reduce-scatter.14.cloned.1.call-update) | async-done | bytes 1296 | tf_op jit(solution)/shard_map/reduce_scatter | solution.py:310
  1222.0 133.5 %reduce-scatter.16.cloned.1.call-done = f32[16,512]{1,0:T(8,128)} async-done(((f32[512,512]{1,0:T(8,128)}), f32[16,512]{1,0:T(8,128)}) %reduce-scatter.16.cloned.1.call-update) | async-done | bytes 32784 | tf_op jit(solution)/shard_map/reduce_scatter | solution.py:316
  1355.6 133.4 %reduce-scatter.22.cloned.1.call-done = f32[16,512]{1,0:T(8,128)} async-done(((f32[512,512]{1,0:T(8,128)}), f32[16,512]{1,0:T(8,128)}) %reduce-scatter.22.cloned.1.call-update) | async-done | bytes 32784
  1489.0 133.5 %reduce-scatter.24.cloned.1.call-done = f32[16,512]{1,0:T(8,128)} async-done(((f32[512,512]{1,0:T(8,128)}), f32[16,512]{1,0:T(8,128)}) %reduce-scatter.24.cloned.1.call-update) | async-done | bytes 32784
  1622.5 133.5 %reduce-scatter.26.cloned.1.call-done = f32[16,512]{1,0:T(8,128)} async-done(((f32[512,512]{1,0:T(8,128)}), f32[16,512]{1,0:T(8,128)}) %reduce-scatter.26.cloned.1.call-update) | async-done | bytes 32784
  1756.0 139.8 %reduce-scatter.18.cloned.1.call-done = f32[16,2048]{1,0:T(8,128)} async-done(((f32[512,2048]{1,0:T(8,128)}), f32[16,2048]{1,0:T(8,128)}) %reduce-scatter.18.cloned.1.call-update) | async-done | bytes 131088 | tf_op jit(solution)/shard_map/reduce_scatter | solution.py:320
  1895.9 139.6 %reduce-scatter.20.cloned.1.call-done = f32[64,512]{1,0:T(8,128)} async-done(((f32[2048,512]{1,0:T(8,128)}), f32[64,512]{1,0:T(8,128)}) %reduce-scatter.20.cloned.1.call-update) | async-done | bytes 131088 | tf_op jit(solution)/shard_map/reduce_scatter | solution.py:322
  (366 shorter events, 178.9 us)
Async XLA Ops:
  7.2 515.0 %all-gather.3.cloned.1.call-start = ((), (), s32[]{:S(2)}) async-start(), calls=%async_computation.7 | async-start | bytes 2162688 | tf_op jit(solution)/shard_map/all_gather | solution.py:99
  7.9 560.8 %all-gather.5.cloned.1.call-start = ((), (), s32[]{:S(2)}) async-start(), calls=%async_computation.8 | async-start | bytes 2162688 | tf_op jit(solution)/shard_map/all_gather | solution.py:101
  8.0 217.5 %collective-permute-start = (bf16[1,16,512]{2,1,0:T(8,128)(2,1)}, bf16[1,16,512]{2,1,0:T(8,128)(2,1)S(1)}, u32[]{:S(2)}, u32[]{:S(2)}) collective-permute-start(bf16[1,16,512]{2,1,0:T(8,128)(2,1)} %bitcast.253), channel_id=1, source_target_pairs={{0,1},{1,0},{2,3},{3,2},{4,5},{5,4},{6,7},{7,6},{8,9},{9,8},{10,11... | collective-permute-start | bytes 49160 | tf_op jit(solution)/shard_map/ppermute | solution.py:24
  8.7 1213.4 %reduce-scatter.14.cloned.1.call-start = ((), (), s32[]{:S(2)}) async-start(), calls=%async_computation.9 | async-start | bytes 270336 | tf_op jit(solution)/shard_map/reduce_scatter | solution.py:310
  100.0 127.2 %copy-start.23 = (bf16[20,512]{0,1:T(8,128)(2,1)}, bf16[20,512]{0,1:T(8,128)(2,1)S(1)}, u32[]{:S(2)}) copy-start(bf16[20,512]{0,1:T(8,128)(2,1)S(1)} %all_gather.59) | copy-start | bytes 61444
  138.8 88.4 %copy-start.19 = (bf16[512,512]{1,0:T(8,128)(2,1)}, bf16[512,512]{1,0:T(8,128)(2,1)S(1)}, u32[]{:S(2)}) copy-start(bf16[512,512]{1,0:T(8,128)(2,1)S(1)} %all_gather.58) | copy-start | bytes 1572868
  178.5 46.8 %copy-start.13 = (bf16[512,512]{1,0:T(8,128)(2,1)}, bf16[512,512]{1,0:T(8,128)(2,1)S(1)}, u32[]{:S(2)}) copy-start(bf16[512,512]{1,0:T(8,128)(2,1)S(1)} %all_gather.60) | copy-start | bytes 1572868
  222.5 7.1 copy-start.46
  225.5 4.0 collective-permute-start.1
  229.5 14.5 collective-permute-start.2
  244.7 209.1 %collective-permute-start.3 = (bf16[8,16,512]{2,1,0:T(8,128)(2,1)}, bf16[8,16,512]{2,1,0:T(8,128)(2,1)}, u32[]{:S(2)}, u32[]{:S(2)}) collective-permute-start(bf16[8,16,512]{2,1,0:T(8,128)(2,1)} %bitcast.18), channel_id=1, source_target_pairs={{0,8},{1,9},{2,10},{3,11},{4,12},{5,13},{6,14},{7,15},{8,0},{9,1},... | collective-permute-start | bytes 393224 | tf_op jit(solution)/shard_map/ppermute | solution.py:24
  453.7 13.5 copy-start.1
  453.7 7.4 copy-start.68
  453.7 7.4 copy-start.67
  453.7 8.0 copy-start.66
  453.7 8.0 copy-start.65
  453.8 8.0 copy-start.64
  453.8 8.6 copy-start.63
  453.8 9.2 copy-start.57
  455.2 61.9 %collective-permute-start.4 = (bf16[16,16,512]{2,1,0:T(8,128)(2,1)S(1)}, bf16[16,16,512]{2,1,0:T(8,128)(2,1)S(1)}, u32[]{:S(2)}, u32[]{:S(2)}) collective-permute-start(bf16[16,16,512]{2,1,0:T(8,128)(2,1)S(1)} %bitcast.245), channel_id=1, source_target_pairs={{0,16},{1,17},{2,18},{3,19},{4,20},{5,21},{6,22},{7,23},{8,24},{9,... | collective-permute-start | bytes 786440 | tf_op jit(solution)/shard_map/ppermute | solution.py:24
  461.2 163.8 %copy-start.55 = (f32[512]{0:T(512)}, f32[512]{0:T(512)S(1)}, u32[]{:S(2)}) copy-start(f32[512]{0:T(512)S(1)} %convert_element_type.158) | copy-start | bytes 6148
  461.8 106.9 %copy-start.60 = (f32[512]{0:T(512)}, f32[512]{0:T(512)S(1)}, u32[]{:S(2)}) copy-start(f32[512]{0:T(512)S(1)} %convert_element_type.159) | copy-start | bytes 6148
  470.5 46.8 %copy-start.31 = (bf16[2048,512]{0,1:T(8,128)(2,1)S(1)}, bf16[2048,512]{0,1:T(8,128)(2,1)}, u32[]{:S(2)}) copy-start(bf16[2048,512]{0,1:T(8,128)(2,1)} %copy.80) | copy-start | bytes 6291460
  471.2 47.8 %copy-start.30 = (bf16[64,8,4,512]{3,1,2,0:T(8,128)(2,1)}, bf16[64,8,4,512]{3,1,2,0:T(8,128)(2,1)S(1)}, u32[]{:S(2)}) copy-start(bf16[64,8,4,512]{3,1,2,0:T(8,128)(2,1)S(1)} %copy.118) | copy-start | bytes 6291460
  519.0 106.0 %copy-start.40 = (f32[2048]{0:T(1024)}, f32[2048]{0:T(1024)S(1)}, u32[]{:S(2)}) copy-start(f32[2048]{0:T(1024)S(1)} %broadcast_multiply_fusion.1) | copy-start | bytes 24580
  522.1 102.9 %copy-start.47 = (f32[2048]{0:T(1024)}, f32[2048]{0:T(1024)S(1)}, u32[]{:S(2)}) copy-start(f32[2048]{0:T(1024)S(1)} %fusion.72) | copy-start | bytes 24580
  522.1 46.6 %copy-start.62 = (f32[512]{0:T(512)S(1)}, f32[512]{0:T(512)}, u32[]{:S(2)}) copy-start(f32[512]{0:T(512)} %convert_element_type.163) | copy-start | bytes 6148
  568.7 11.2 copy-start.8
  568.7 11.2 copy-start.44
  568.7 11.2 copy-start.45
  579.8 4.7 copy-start.5
  612.0 12.9 copy-start.39
  612.0 13.0 copy-start.11
  635.8 7.2 copy-start.2
  635.8 7.2 copy-start.21
  635.8 7.2 copy-start.22
  635.8 7.2 copy-start.34
  643.2 6.8 copy-start.4
  733.4 10.9 copy-start
  744.4 6.3 copy-start.3
  752.6 6.8 copy-start.4
  844.1 10.9 copy-start
  855.0 7.6 copy-start.3
  864.6 6.8 copy-start.4
  956.0 10.9 copy-start
  966.9 7.6 copy-start.3
  976.5 6.8 copy-start.4
  1067.9 10.9 copy-start
  1078.8 7.6 copy-start.3
  1092.3 4.8 copy-start.9
  1092.3 263.3 %reduce-scatter.16.cloned.1.call-start = ((), (), s32[]{:S(2)}) async-start(), calls=%async_computation.10 | async-start | bytes 1081344 | tf_op jit(solution)/shard_map/reduce_scatter | solution.py:316
  1097.0 392.0 %reduce-scatter.22.cloned.1.call-start = ((), (), s32[]{:S(2)}) async-start(), calls=%async_computation.13 | async-start | bytes 1081344
  1103.3 519.2 %reduce-scatter.24.cloned.1.call-start = ((), (), s32[]{:S(2)}) async-start(), calls=%async_computation.14 | async-start | bytes 1081344
  1110.3 645.8 %reduce-scatter.26.cloned.1.call-start = ((), (), s32[]{:S(2)}) async-start(), calls=%async_computation.15 | async-start | bytes 1081344
  1117.3 778.6 %reduce-scatter.18.cloned.1.call-start = ((), (), s32[]{:S(2)}) async-start(), calls=%async_computation.11 | async-start | bytes 4325376 | tf_op jit(solution)/shard_map/reduce_scatter | solution.py:320
  1128.6 906.9 %reduce-scatter.20.cloned.1.call-start = ((), (), s32[]{:S(2)}) async-start(), calls=%async_computation.12 | async-start | bytes 4325376 | tf_op jit(solution)/shard_map/reduce_scatter | solution.py:322
  1139.5 4.5 copy-start.20
  1153.4 5.4 copy-start.49
  1153.4 5.4 copy-start.50
  1153.4 5.4 copy-start.51
  1153.4 5.4 copy-start.52
  1153.4 5.4 copy-start.54
  1153.4 5.4 copy-start.58
  1153.5 5.4 copy-start.59
  (28 other events, 72.5 us)
Sparse Core Ops, SparseCore 0:
  10.9 59.2 all-gather.2
  73.0 55.7 all-gather.4
  1092.4 129.5 reduce-scatter.13
  1224.8 130.7 reduce-scatter.15
  1358.2 130.7 reduce-scatter.21
  1491.8 130.7 reduce-scatter.23
  1625.3 130.6 reduce-scatter.25
  1759.0 136.8 reduce-scatter.17
  1898.8 136.6 reduce-scatter.19
